TPU v7x, 32 devices: a whole 2x2x4 slice. The times are simulated.
32 devices in a mesh: dp: 4 (over x, core), seq: 8 (over z, y).
Axes of the slice: x: 2, y: 2, z: 4, core: 2. Of those that a mesh axis runs over, the one named last changes fastest.
Arguments:
- queries: bfloat16 [4, 1024, 1024], P('dp', 'seq'), may hold values from -40 to 40
- key_rows: bfloat16 [4, 1024, 1024], P('dp', 'seq'), may hold values from -9 to 9
- value_rows: bfloat16 [4, 1024, 1024], P('dp', 'seq'), may hold values from -6 to 6
- query_tangent: bfloat16 [4, 1024, 1024], P('dp', 'seq'), may hold values from -6 to 6
- key_tangent: bfloat16 [4, 1024, 1024], P('dp', 'seq'), may hold values from -6 to 6
- value_tangent: bfloat16 [4, 1024, 1024], P('dp', 'seq'), may hold values from -6 to 6
- out_weight: bfloat16 [1024, 2048], replicated, may hold values from -0.75 to 0.75
- upstream: bfloat16 [4, 1024, 2048], P('dp', 'seq'), may hold values from -6 to 6
Outputs:
- block_out: bfloat16 [4, 1024, 2048], P('dp', 'seq')
- tangent_out: bfloat16 [4, 1024, 2048], P('dp', 'seq')
- grad_weight: float32 [1024, 2048], P(('dp', 'seq'))
- grad_query: bfloat16 [4, 1024, 1024], P('dp', 'seq')
- grad_key: bfloat16 [4, 1024, 1024], P('dp', 'seq')
- grad_value: bfloat16 [4, 1024, 1024], P('dp', 'seq')
All inputs are finite; a program needn't handle non-finite values.
Results may differ from a plain program's by a relative error of at most 0.035.
Values may be sent and summed in bfloat16 or wider, within the bound.
A program may use at most 192 MiB of HBM per device.

v0:
```python
import math

import jax
import jax.numpy as jnp
from jax import lax
from jax.sharding import PartitionSpec as P

HEADS = 8
HEAD_DIM = 128


def to_heads(matrix):
    return matrix.reshape(matrix.shape[0], HEADS, HEAD_DIM)


def per_device(
    queries, key_rows, value_rows, query_tangent, key_tangent, value_tangent, out_weight, upstream
):
    local_q = to_heads(queries[0])
    local_tq = to_heads(query_tangent[0])
    tokens = queries.shape[1]
    attn_width = queries.shape[2]
    full_len = tokens * lax.axis_size("seq")
    softmax_scale = HEAD_DIM ** (-0.5)
    head_zeros = jnp.zeros((HEADS, tokens), jnp.float32)
    acc_zeros = jnp.zeros((tokens, HEADS, HEAD_DIM), jnp.float32)
    run_max = jnp.full((HEADS, tokens), -jnp.inf, jnp.float32)
    run_sum = head_zeros
    run_tan = head_zeros
    acc_main = acc_zeros
    acc_tan = acc_zeros
    key_piece = lax.all_gather(key_rows[0], "seq", axis=0, tiled=True)
    value_piece = lax.all_gather(value_rows[0], "seq", axis=0, tiled=True)
    key_tan_piece = lax.all_gather(key_tangent[0], "seq", axis=0, tiled=True)
    value_tan_piece = lax.all_gather(value_tangent[0], "seq", axis=0, tiled=True)
    key_heads = to_heads(key_piece)
    value_heads = to_heads(value_piece)
    key_tan_heads = to_heads(key_tan_piece)
    value_tan_heads = to_heads(value_tan_piece)
    scores = (
        jnp.einsum("thd,shd->hts", local_q, key_heads, preferred_element_type=jnp.float32)
        * softmax_scale
    )
    tan_scores = (
        jnp.einsum("thd,shd->hts", local_tq, key_heads, preferred_element_type=jnp.float32)
        + jnp.einsum("thd,shd->hts", local_q, key_tan_heads, preferred_element_type=jnp.float32)
    ) * softmax_scale
    new_max = jnp.max(scores, axis=2)
    shrink = jnp.exp(run_max - new_max)
    exp_scores = jnp.exp(scores - new_max[:, :, None])
    weighted = exp_scores * tan_scores
    run_sum = run_sum * shrink + jnp.sum(exp_scores, axis=2)
    run_tan = run_tan * shrink + jnp.sum(weighted, axis=2)
    exp_low = exp_scores.astype(jnp.bfloat16)
    weighted_low = weighted.astype(jnp.bfloat16)
    shrink_rows = shrink.T[:, :, None]
    acc_main = acc_main * shrink_rows + jnp.einsum(
        "hts,shd->thd", exp_low, value_heads, preferred_element_type=jnp.float32
    )
    acc_tan = (
        acc_tan * shrink_rows
        + jnp.einsum("hts,shd->thd", weighted_low, value_heads, preferred_element_type=jnp.float32)
        + jnp.einsum("hts,shd->thd", exp_low, value_tan_heads, preferred_element_type=jnp.float32)
    )
    key_store = key_piece
    value_store = value_piece
    folded = (new_max, run_sum, run_tan, acc_main, acc_tan, key_store, value_store)
    run_max, run_sum, run_tan, acc_main, acc_tan, key_store, value_store = folded
    sum_rows = run_sum.T[:, :, None]
    attn_wide = acc_main / sum_rows
    attn = attn_wide.astype(jnp.bfloat16)
    tan_attn = ((acc_tan - attn_wide * run_tan.T[:, :, None]) / sum_rows).astype(jnp.bfloat16)
    log_total = run_max + jnp.log(run_sum)
    attn_flat = attn.reshape(tokens, attn_width)
    tan_flat = tan_attn.reshape(tokens, attn_width)
    block_wide = jnp.dot(attn_flat, out_weight, preferred_element_type=jnp.float32)
    tan_wide = jnp.dot(tan_flat, out_weight, preferred_element_type=jnp.float32)
    cotangent = (tan_wide + upstream[0].astype(jnp.float32)).astype(jnp.bfloat16)
    grad_attn = jnp.einsum(
        "te,ke->tk", cotangent, out_weight, preferred_element_type=jnp.float32
    ).astype(jnp.bfloat16)
    grad_factor = 1.0 / math.sqrt(lax.axis_size("dp") * full_len)
    grad_heads = to_heads(grad_attn)
    row_delta = jnp.einsum("thd,thd->ht", grad_heads, attn, preferred_element_type=jnp.float32)
    key_all = to_heads(key_store)
    value_all = to_heads(value_store)
    scores_all = (
        jnp.einsum("thd,shd->hts", local_q, key_all, preferred_element_type=jnp.float32)
        * softmax_scale
    )
    attn_prob = jnp.exp(scores_all - log_total[:, :, None])
    grad_prob = jnp.einsum(
        "thd,shd->hts", grad_heads, value_all, preferred_element_type=jnp.float32
    )
    grad_scores = (attn_prob * (grad_prob - row_delta[:, :, None])).astype(jnp.bfloat16)
    grad_query = (
        softmax_scale
        * jnp.einsum("hts,shd->thd", grad_scores, key_all, preferred_element_type=jnp.float32)
    ).astype(jnp.bfloat16)
    all_lse, all_delta = (
        lax.all_gather(log_total.T, "seq", axis=0, tiled=True),
        lax.all_gather(row_delta.T, "seq", axis=0, tiled=True),
    )
    own_keys = to_heads(key_rows[0])
    own_values = to_heads(value_rows[0])
    query_piece = lax.all_gather(queries[0], "seq", axis=0, tiled=True)
    grad_piece = lax.all_gather(grad_attn, "seq", axis=0, tiled=True)
    query_heads = to_heads(query_piece)
    grad_piece_heads = to_heads(grad_piece)
    scores_piece = (
        jnp.einsum("qhd,khd->hqk", query_heads, own_keys, preferred_element_type=jnp.float32)
        * softmax_scale
    )
    prob_piece = jnp.exp(scores_piece - all_lse.T[:, :, None])
    dprob = jnp.einsum(
        "qhd,khd->hqk", grad_piece_heads, own_values, preferred_element_type=jnp.float32
    )
    dscore = (prob_piece * (dprob - all_delta.T[:, :, None])).astype(jnp.bfloat16)
    key_grad_sum = softmax_scale * jnp.einsum(
        "hqk,qhd->khd", dscore, query_heads, preferred_element_type=jnp.float32
    )
    value_grad_sum = jnp.einsum(
        "hqk,qhd->khd",
        prob_piece.astype(jnp.bfloat16),
        grad_piece_heads,
        preferred_element_type=jnp.float32,
    )
    grad_key = key_grad_sum.reshape(tokens, attn_width).astype(jnp.bfloat16)
    grad_value = value_grad_sum.reshape(tokens, attn_width).astype(jnp.bfloat16)
    grad_weight = lax.psum_scatter(
        grad_factor
        * jnp.einsum("tk,te->ke", attn_flat, cotangent, preferred_element_type=jnp.float32),
        ("dp", "seq"),
        scatter_dimension=0,
        tiled=True,
    )
    return (
        block_wide.astype(jnp.bfloat16)[None],
        tan_wide.astype(jnp.bfloat16)[None],
        grad_weight,
        grad_query.reshape(tokens, attn_width)[None],
        grad_key[None],
        grad_value[None],
    )


def solution(mesh):
    placed = (
        P("dp", "seq", None),
        P("dp", "seq", None),
        P("dp", "seq", None),
        P("dp", "seq", None),
        P("dp", "seq", None),
        P("dp", "seq", None),
        P(),
        P("dp", "seq", None),
    )
    return jax.shard_map(
        per_device,
        mesh=mesh,
        in_specs=placed,
        out_specs=(
            P("dp", "seq", None),
            P("dp", "seq", None),
            P(("dp", "seq"), None),
            P("dp", "seq", None),
            P("dp", "seq", None),
            P("dp", "seq", None),
        ),
        check_vma=False,
    )
```

profile of v0, /device:TPU:0, one launch (start us, length us, event | category | flops | bytes accessed | tf_op | source)
XLA Modules:
  0.0 510.6 jit_solution(4488114547898014484)
XLA Ops:
  7.2 1.8 copy.26
  10.6 1.8 copy.32
  12.4 1.8 copy.36
  16.3 48.1 %all-gather.14.cloned.1.call-done = bf16[1,1024,1024]{1,2,0:T(8,128)(2,1)} async-done(((bf16[1,128,1024]{1,2,0:T(8,128)(2,1)}), bf16[1,1024,1024]{1,2,0:T(8,128)(2,1)}) %all-gather.14.cloned.1.call-update) | async-done | bytes 2097168 | tf_op jit(solution)/shard_map/all_gather | solution.py:32
  64.4 4.3 multiply_reduce_fusion
  68.7 45.4 %all-gather.16.cloned.1.call-done = bf16[1,1024,1024]{2,1,0:T(8,128)(2,1)} async-done(((bf16[1,128,1024]{2,1,0:T(8,128)(2,1)}), bf16[1,1024,1024]{2,1,0:T(8,128)(2,1)}) %all-gather.16.cloned.1.call-update) | async-done | bytes 2097168 | tf_op jit(solution)/shard_map/all_gather | solution.py:33
  114.1 3.9 copy.29
  118.0 46.0 %all-gather.20.cloned.1.call-done = bf16[1,1024,1024]{2,1,0:T(8,128)(2,1)} async-done(((bf16[1,128,1024]{2,1,0:T(8,128)(2,1)}), bf16[1,1024,1024]{2,1,0:T(8,128)(2,1)}) %all-gather.20.cloned.1.call-update) | async-done | bytes 2097168 | tf_op jit(solution)/shard_map/all_gather | solution.py:35
  164.0 4.0 copy.35
  168.0 3.1 fusion.1
  171.0 2.7 fusion.40
  173.7 42.4 %all-gather.18.cloned.1.call-done = bf16[1,1024,1024]{1,2,0:T(8,128)(2,1)} async-done(((bf16[1,128,1024]{1,2,0:T(8,128)(2,1)}), bf16[1,1024,1024]{1,2,0:T(8,128)(2,1)}) %all-gather.18.cloned.1.call-update) | async-done | bytes 2097168 | tf_op jit(solution)/shard_map/all_gather | solution.py:34
  216.1 5.8 %fusion.54 = (f32[8,128]{1,0:T(8,128)S(1)}, bf16[8,128,1024]{2,1,0:T(8,128)(2,1)S(1)}) fusion(f32[8,128,1024]{2,1,0:T(8,128)} %fusion.40, bf16[1024,8,128]{0,2,1:T(8,128)(2,1)} %bitcast.130, bf16[128,8,128]{2,1,0:T(8,128)(2,1)S(1)} %bitcast.125, f32[8,128]{1,0:T(8,128)S(1)} %get-tuple-element.24, f32[8,128,1024]{2,1,0:T(8,128)} %get-tuple-element.25), kind=kOutput, calls=%fused_computation.61 | convolution fusion | flops 275774464 | bytes 12853248 | tf_op jit(solution)/shard_map/thd,shd->hts/dot_general | solution.py:46
  222.6 1.6 copy-done.1
  224.2 1.2 fusion.16
  225.4 1.2 fusion.25
  228.5 2.3 convolution_convert_fusion.1
  232.9 2.0 copy.52
  234.9 1.3 multiply_reduce_fusion.1
  236.2 5.5 %convolution_multiply_fusion = f32[1024,2048]{1,0:T(8,128)} fusion(bf16[128,1024]{0,1:T(8,128)(2,1)S(1)} %bitcast.122, f32[128,2048]{1,0:T(8,128)S(1)} %fusion.55, bf16[1,128,2048]{2,1,0:T(8,128)(2,1)} %param.15), kind=kOutput, calls=%fused_computation | convolution fusion | flops 539754496 | bytes 10223616 | tf_op jit(solution)/shard_map/tk,te->ke/dot_general | solution.py:132
  241.7 1.8 copy.56
  243.5 1.7 copy.62
  245.3 5.6 %fusion.26 = bf16[8,128,128]{1,2,0:T(8,128)(2,1)} fusion(bf16[1024,8,128]{0,2,1:T(8,128)(2,1)S(1)} %bitcast.118, f32[8,128,1024]{2,1,0:T(8,128)} %get-tuple-element.25, bf16[1024,8,128]{0,2,1:T(8,128)(2,1)} %bitcast.119, f32[8,128]{1,0:T(8,128)S(1)} %get-tuple-element.18, f32[8,128]{1,0:T(8,128)S(1)} %log_add_fusion, ...), kind=kOutput, calls=%fused_computation.31 | convolution fusion | flops 542375936 | bytes 8921088 | tf_op jit(solution)/shard_map/hts,shd->thd/dot_general | solution.py:98
  250.9 1.8 copy.40
  252.7 30.5 %all_gather.31 = f32[1024,8]{0,1:T(8,128)S(1)} all-gather(f32[128,8]{0,1:T(8,128)S(1)} %bitcast.144), channel_id=1, replica_groups=mesh['dp'=4,'seq'=8] {'seq'}, dimensions={0}, use_global_device_ids=true | all-gather | bytes 36864 | tf_op jit(solution)/shard_map/all_gather | solution.py:102
  283.2 30.6 %all_gather.29 = f32[1024,8]{0,1:T(8,128)S(1)} all-gather(f32[128,8]{0,1:T(8,128)S(1)} %get-tuple-element.20), channel_id=1, replica_groups=mesh['dp'=4,'seq'=8] {'seq'}, dimensions={0}, use_global_device_ids=true | all-gather | bytes 36864 | tf_op jit(solution)/shard_map/all_gather | solution.py:101
  313.8 3.7 fusion.3
  317.6 4.4 fusion.38
  322.8 2.9 copy.57
  325.7 5.8 %fusion.27 = bf16[8,128,128]{1,2,0:T(8,128)(2,1)S(1)} fusion(bf16[1024,8,128]{0,2,1:T(8,128)(2,1)} %bitcast.128, f32[8,1024,128]{2,1,0:T(8,128)} %fusion.38, bf16[1024,8,128]{0,2,1:T(8,128)(2,1)S(1)} %bitcast.114, bf16[128,8,128]{0,2,1:T(8,128)(2,1)S(1)} %bitcast.137, f32[8,1024]{1,0:T(8,128)S(1)} %bitcast.143, f32[8,1024]{1,0:T(8,128)S(1)} %bitcast.141), kind=kOutput, calls=%fused_computation.32 | convolution fusion | flops 542375936 | bytes 8978432 | tf_op jit(solution)/shard_map/hqk,qhd->khd/dot_general | solution.py:119
  332.4 3.3 fusion.28
  336.6 167.1 %reduce-scatter.2.cloned.1.call-done = f32[32,2048]{1,0:T(8,128)} async-done(((f32[1024,2048]{1,0:T(8,128)}), f32[32,2048]{1,0:T(8,128)}) %reduce-scatter.2.cloned.1.call-update) | async-done | bytes 262160 | tf_op jit(solution)/shard_map/reduce_scatter | solution.py:130
  (44 shorter events, 10.9 us)
Async XLA Ops:
  7.2 57.3 %all-gather.14.cloned.1.call-start = ((), (), s32[]{:S(2)}) async-start(), calls=%async_computation.3 | async-start | bytes 2359296 | tf_op jit(solution)/shard_map/all_gather | solution.py:32
  9.0 105.0 %all-gather.16.cloned.1.call-start = ((), (), s32[]{:S(2)}) async-start(), calls=%async_computation.4 | async-start | bytes 2359296 | tf_op jit(solution)/shard_map/all_gather | solution.py:33
  9.8 154.2 %all-gather.20.cloned.1.call-start = ((), (), s32[]{:S(2)}) async-start(), calls=%async_computation.6 | async-start | bytes 2359296 | tf_op jit(solution)/shard_map/all_gather | solution.py:35
  10.5 205.5 %all-gather.18.cloned.1.call-start = ((), (), s32[]{:S(2)}) async-start(), calls=%async_computation.5 | async-start | bytes 2359296 | tf_op jit(solution)/shard_map/all_gather | solution.py:34
  12.4 305.2 %all-gather.22.cloned.1.call-start = ((), (), s32[]{:S(2)}) async-start(), calls=%async_computation.7 | async-start | bytes 2359296 | tf_op jit(solution)/shard_map/all_gather | solution.py:106
  14.2 308.6 %all-gather.12.cloned.1.call-start = ((), (), s32[]{:S(2)}) async-start(), calls=%async_computation.2 | async-start | bytes 2359296 | tf_op jit(solution)/shard_map/all_gather | solution.py:107
  118.0 53.0 %copy-start.2 = (bf16[1,1024,1024]{1,2,0:T(8,128)(2,1)S(1)}, bf16[1,1024,1024]{1,2,0:T(8,128)(2,1)}, u32[]{:S(2)}) copy-start(bf16[1,1024,1024]{1,2,0:T(8,128)(2,1)} %all-gather.14.cloned.1.call-done) | copy-start | bytes 6291460
  216.1 5.8 %copy-start.3 = (bf16[1,1024,1024]{1,2,0:T(8,128)(2,1)S(1)}, bf16[1,1024,1024]{1,2,0:T(8,128)(2,1)}, u32[]{:S(2)}) copy-start(bf16[1,1024,1024]{1,2,0:T(8,128)(2,1)} %copy.29) | copy-start | bytes 6291460
  221.8 2.3 copy-start.1
  222.6 2.8 copy-start.5
  225.3 1.3 copy-start.7
  225.4 2.4 copy-start
  226.6 1.9 copy-start.4
  230.8 272.9 %reduce-scatter.2.cloned.1.call-start = ((), (), s32[]{:S(2)}) async-start(), calls=%async_computation.1 | async-start | bytes 8650752 | tf_op jit(solution)/shard_map/reduce_scatter | solution.py:130
  250.9 66.7 %copy-start.6 = (bf16[16,8,8,128]{3,2,1,0:T(8,128)(2,1)S(1)}, bf16[16,8,8,128]{3,2,1,0:T(8,128)(2,1)}, u32[]{:S(2)}) copy-start(bf16[16,8,8,128]{3,2,1,0:T(8,128)(2,1)} %copy.62) | copy-start | bytes 786436
  321.9 3.8 copy-start.8
Sparse Core Ops, SparseCore 0:
  10.6 53.7 all-gather.13
  66.5 47.4 all-gather.15
  116.2 47.7 all-gather.19
  166.5 49.5 all-gather.17
  218.0 49.4 all-gather.21
  270.0 47.5 all-gather.11
  320.5 183.2 reduce-scatter.1
where the time goes:
time: 511 us
  waiting for transfers between devices  350 us (68%)
  blocking collectives  61.1 us (12%)
  matrix products  47.2 us (9%)
  local copies, waits for them, and re-layouts  31 us (6%)
  between operations  14.3 us (3%)
  other arithmetic  6.06 us (1%)
    reduce_scatter x1, waiting for transfers between devices, per_device(): lax.psum_scatter(grad_factor * jnp.einsum('tk,te->ke', attn_flat, cotange...  167 us
    all_gather x1, waiting for transfers between devices, per_device(): key_piece = lax.all_gather(key_rows[0], 'seq', axis=0, tiled=True)  48.1 us
    all_gather x1, waiting for transfers between devices, per_device(): lax.all_gather(value_tangent[0], 'seq', axis=0, tiled=True)  46 us
    all_gather x1, waiting for transfers between devices, per_device(): value_piece = lax.all_gather(value_rows[0], 'seq', axis=0, tiled=True)  45.4 us
    all_gather x1, waiting for transfers between devices, per_device(): key_tan_piece = lax.all_gather(key_tangent[0], 'seq', axis=0, tiled=True)  42.4 us
    all_gather x1, blocking collectives, per_device(): lax.all_gather(log_total.T, 'seq', axis=0, tiled=True)  30.6 us
    all_gather x1, blocking collectives, per_device(): lax.all_gather(row_delta.T, 'seq', axis=0, tiled=True)  30.5 us
    unnamed x29, local copies, waits for them, and re-layouts  18.3 us
  transfers between devices with their start and end apart: 7, of which 5 were waited for; matrix products, arithmetic and copies ran while one was open for 16% of the time, Pallas kernels for 0%

commit v1 on v0

--- a/solution.py
+++ b/solution.py
@@ -1,8 +1,11 @@
+import functools
 import math
 
 import jax
 import jax.numpy as jnp
 from jax import lax
+from jax.experimental import pallas as pl
+from jax.experimental.pallas import tpu as pltpu
 from jax.sharding import PartitionSpec as P
 
 HEADS = 8
@@ -144,7 +147,398 @@
     )
 
 
+MESH = pl.DeviceIdType.MESH
+NT = (((1,), (1,)), ((), ()))
+TN = (((0,), (0,)), ((), ()))
+
+
+def dotf(a, b, dims=(((1,), (0,)), ((), ()))):
+    return lax.dot_general(a, b, dims, preferred_element_type=jnp.float32)
+
+
+def fused_kernel(
+    n, ndp, q_ref, k_ref, v_ref, tq_ref, tk_ref, tv_ref, w_hbm, up_hbm,
+    block_ref, tan_ref, gw_ref, gq_out, gk_out, gv_out,
+    qq, kk, vv, prob, attn_own, tan_own, attn_full, tan_full, w_ref, up_ref,
+    cots, attn_dp, grad_loc, grad_own, gq_acc, gq_st, gk_st, gv_st, gw_st, gw_land,
+    in_send, in_recv, fw_send, fw_recv, g_send, g_recv, gr_send, gr_recv,
+    gw_send, gw_recv, cot_send, cot_recv, ad_send, ad_recv, load_sem,
+):
+    dp, me = lax.axis_index("dp"), lax.axis_index("seq")
+    tok = q_ref.shape[0]
+    hd = HEAD_DIM
+    full = n * tok
+    rows_dp = gw_st.shape[0]
+    rows_own = rows_dp // n
+    scale = HEAD_DIM ** (-0.5)
+    gw_scale = 1.0 / math.sqrt(ndp * full)
+    dp_peers = [dp, dp + 1 - 2 * lax.rem(dp, 2), lax.rem(dp + 2, 4), 3 - dp]
+
+    def peer(d):
+        return lax.rem(me + d, n)
+
+    def source(d):
+        return lax.rem(me + n - d, n)
+
+    def at(i, size):
+        return pl.ds(pl.multiple_of(i * size, size), size)
+
+    barrier = pltpu.get_barrier_semaphore()
+    for d in range(1, n):
+        pl.semaphore_signal(barrier, inc=1, device_id=(dp, peer(d)), device_id_type=MESH)
+    for j in range(1, ndp):
+        pl.semaphore_signal(barrier, inc=1, device_id=(dp_peers[j], me), device_id_type=MESH)
+
+    load_w = pltpu.make_async_copy(w_hbm, w_ref, load_sem.at[0])
+    load_up = pltpu.make_async_copy(up_hbm, up_ref, load_sem.at[1])
+
+    arrivals = (
+        (q_ref, qq, 1), (k_ref, kk, 0), (tq_ref, qq, 0),
+        (tk_ref, kk, 1), (v_ref, vv, 0), (tv_ref, vv, 1),
+    )
+
+    def in_copy(a, to, owner, d):
+        src, dst, side = arrivals[a]
+        return pltpu.make_async_remote_copy(
+            src_ref=src.at[:, at(to, hd)],
+            dst_ref=dst.at[at(owner, tok), pl.ds(side * hd, hd)],
+            send_sem=in_send.at[a, d], recv_sem=in_recv.at[a, d],
+            device_id=(dp, to), device_id_type=MESH,
+        )
+
+    def in_local(a):
+        src, dst, side = arrivals[a]
+        return pltpu.make_async_copy(
+            src.at[:, at(me, hd)], dst.at[at(me, tok), pl.ds(side * hd, hd)], in_recv.at[a, 0]
+        )
+
+    for a in range(6):
+        in_local(a).start()
+    pl.semaphore_wait(barrier, n - 1 + ndp - 1)
+    for a in range(6):
+        @pl.loop(1, n)
+        def _(d):
+            in_copy(a, peer(d), me, d).start()
+    load_w.start()
+    load_up.start()
+
+    def in_wait(a):
+        in_local(a).wait()
+
+        @pl.loop(1, n)
+        def _(d):
+            in_copy(a, source(d), source(d), d).wait_recv()
+
+    for a in range(6):
+        in_wait(a)
+
+    def fw_copy(i, to, owner, d):
+        src, dst = ((attn_own, attn_full), (tan_own, tan_full))[i]
+        return pltpu.make_async_remote_copy(
+            src_ref=src.at[at(to, tok), :],
+            dst_ref=dst.at[:, at(owner, hd)],
+            send_sem=fw_send.at[i, d], recv_sem=fw_recv.at[i, d],
+            device_id=(dp, to), device_id_type=MESH,
+        )
+
+    def fw_local(i):
+        src, dst = ((attn_own, attn_full), (tan_own, tan_full))[i]
+        return pltpu.make_async_copy(
+            src.at[at(me, tok), :], dst.at[:, at(me, hd)], fw_recv.at[i, 0]
+        )
+
+    span = 2 * tok
+    parts = n // 2
+
+    @pl.loop(0, parts)
+    def _(j):
+        p = lax.rem(me // 2 + 1 + j, parts)
+        rows = at(p, span)
+        q2 = qq[rows, :]
+        s = dotf(q2[:, hd:], kk[:, :hd], NT)
+        e = jnp.exp((s - jnp.max(s, axis=1, keepdims=True)) * scale)
+        wgt = e * dotf(q2, kk[...], NT)
+        total = jnp.sum(e, axis=1, keepdims=True)
+        tan_total = jnp.sum(wgt, axis=1, keepdims=True) * scale
+        inv = 1.0 / total
+        both = dotf(e.astype(jnp.bfloat16), vv[...])
+        acc_t = dotf(wgt.astype(jnp.bfloat16), vv[:, :hd]) * scale + both[:, hd:]
+        wide = both[:, :hd] * inv
+        attn_own[rows, :] = wide.astype(jnp.bfloat16)
+        tan_own[rows, :] = ((acc_t - wide * tan_total) * inv).astype(jnp.bfloat16)
+        pb = (e * inv).astype(jnp.bfloat16)
+        for c in range(parts):
+            prob[c, rows, :] = pb[:, c * span:(c + 1) * span]
+        for half in range(2):
+            owner = 2 * p + half
+            d = lax.rem(owner + n - me, n)
+
+            @pl.when(d != 0)
+            def _():
+                fw_copy(1, owner, me, d).start()
+                fw_copy(0, owner, me, d).start()
+
+            @pl.when(d == 0)
+            def _():
+                fw_local(1).start()
+                fw_local(0).start()
+
+    load_w.wait()
+    load_up.wait()
+
+    def fw_wait(i):
+        fw_local(i).wait()
+
+        @pl.loop(1, n)
+        def _(d):
+            fw_copy(i, source(d), source(d), d).wait_recv()
+
+    fw_wait(1)
+    ty = dotf(tan_full[...], w_ref[...])
+    tan_ref[...] = ty.astype(jnp.bfloat16)
+    cot = (ty + up_ref[...].astype(jnp.float32)).astype(jnp.bfloat16)
+    cots[pl.ds(0, tok), :] = cot
+    grad_loc[...] = dotf(cot, w_ref[...], NT).astype(jnp.bfloat16)
+
+    def g_copy(to, owner, d):
+        return pltpu.make_async_remote_copy(
+            src_ref=grad_loc.at[:, at(to, hd)],
+            dst_ref=grad_own.at[at(owner, tok), :],
+            send_sem=g_send.at[d], recv_sem=g_recv.at[d],
+            device_id=(dp, to), device_id_type=MESH,
+        )
+
+    g_local = pltpu.make_async_copy(
+        grad_loc.at[:, at(me, hd)], grad_own.at[at(me, tok), :], g_recv.at[0]
+    )
+    g_local.start()
+
+    @pl.loop(1, n)
+    def _(d):
+        g_copy(peer(d), me, d).start()
+
+    def cot_copy(src_slot, dst_slot, to):
+        return pltpu.make_async_remote_copy(
+            src_ref=cots.at[pl.ds(src_slot * tok, tok), :],
+            dst_ref=cots.at[pl.ds(dst_slot * tok, tok), :],
+            send_sem=cot_send.at[dst_slot], recv_sem=cot_recv.at[dst_slot],
+            device_id=(to, me), device_id_type=MESH,
+        )
+
+    cot_x = cot_copy(0, 2, dp_peers[2])
+    cot_core = cot_copy(0, 1, dp_peers[1])
+    cot_fwd = cot_copy(2, 3, dp_peers[1])
+    cot_x.start()
+    cot_core.start()
+
+    fw_wait(0)
+
+    def ad_copy(j):
+        return pltpu.make_async_remote_copy(
+            src_ref=attn_full.at[:, at(dp_peers[j], rows_dp)],
+            dst_ref=attn_dp.at[pl.ds(j * tok, tok), :],
+            send_sem=ad_send.at[j], recv_sem=ad_recv.at[j],
+            device_id=(dp_peers[j], me), device_id_type=MESH,
+        )
+
+    ad_local = pltpu.make_async_copy(
+        attn_full.at[:, at(dp, rows_dp)], attn_dp.at[pl.ds(0, tok), :], ad_recv.at[0]
+    )
+    for j in range(1, ndp):
+        ad_copy(j).start()
+    ad_local.start()
+    block_ref[...] = dotf(attn_full[...], w_ref[...]).astype(jnp.bfloat16)
+
+    g_local.wait()
+
+    @pl.loop(1, n)
+    def _(d):
+        g_copy(source(d), source(d), d).wait_recv()
+
+    outs = ((gk_st, gk_out), (gv_st, gv_out), (gq_st, gq_out))
+
+    def gr_copy(i, to, owner, d):
+        src, dst = outs[i]
+        return pltpu.make_async_remote_copy(
+            src_ref=src.at[at(to, tok), :],
+            dst_ref=dst.at[:, at(owner, hd)],
+            send_sem=gr_send.at[i, d], recv_sem=gr_recv.at[i, d],
+            device_id=(dp, to), device_id_type=MESH,
+        )
+
+    def gr_local(i):
+        src, dst = outs[i]
+        return pltpu.make_async_copy(
+            src.at[at(me, tok), :], dst.at[:, at(me, hd)], gr_recv.at[i, 0]
+        )
+
+    g_all = grad_own[...]
+    delta = jnp.sum(
+        g_all.astype(jnp.float32) * attn_own[...].astype(jnp.float32), axis=1, keepdims=True
+    )
+    gq_acc[...] = jnp.zeros_like(gq_acc)
+
+    def back_chunk(j):
+        p = lax.rem(me // 2 + 1 + j, parts)
+        rows = at(p, span)
+        pc = prob[p]
+        dprob = dotf(g_all, vv[rows, :hd], NT)
+        ds = (pc.astype(jnp.float32) * (dprob - delta)).astype(jnp.bfloat16)
+        gq_acc[...] += dotf(ds, kk[rows, :hd])
+        gk_st[rows, :] = (dotf(qq[:, hd:], ds, TN).T * scale).astype(jnp.bfloat16)
+        gv_st[rows, :] = dotf(g_all, pc, TN).T.astype(jnp.bfloat16)
+        for half in range(2):
+            owner = 2 * p + half
+            d = lax.rem(owner + n - me, n)
+
+            @pl.when(d != 0)
+            def _():
+                gr_copy(0, owner, me, d).start()
+                gr_copy(1, owner, me, d).start()
+
+            @pl.when(d == 0)
+            def _():
+                gr_local(0).start()
+                gr_local(1).start()
+
+    def gw_copy(to, d):
+        return pltpu.make_async_remote_copy(
+            src_ref=gw_st.at[at(to, rows_own), :],
+            dst_ref=gw_land.at[d],
+            send_sem=gw_send.at[d], recv_sem=gw_recv.at[d],
+            device_id=(dp, to), device_id_type=MESH,
+        )
+
+    first = parts // 2
+
+    @pl.loop(0, first)
+    def _(j):
+        back_chunk(j)
+
+    cot_x.wait_recv()
+    cot_fwd.start()
+    cot_core.wait_recv()
+    ad_local.wait()
+    for j in range(1, ndp):
+        ad_copy(j).wait_recv()
+    cot_fwd.wait_recv()
+    gw_st[...] = (dotf(attn_dp[...], cots[...], TN) * gw_scale).astype(jnp.bfloat16)
+
+    @pl.loop(1, n)
+    def _(d):
+        gw_copy(peer(d), d).start()
+
+    @pl.loop(first, parts)
+    def _(j):
+        back_chunk(j)
+
+    gq_st[...] = (gq_acc[...] * scale).astype(jnp.bfloat16)
+    gr_local(2).start()
+
+    @pl.loop(1, n)
+    def _(d):
+        gr_copy(2, peer(d), me, d).start()
+
+    gw_total = gw_st[at(me, rows_own), :].astype(jnp.float32)
+    for d in range(1, n):
+        gw_copy(source(d), d).wait_recv()
+        gw_total = gw_total + gw_land[d].astype(jnp.float32)
+    gw_ref[...] = gw_total
+
+    for i in range(3):
+        gr_local(i).wait()
+
+        @pl.loop(1, n)
+        def _(d):
+            gr_copy(i, source(d), source(d), d).wait_recv()
+
+    @pl.loop(1, n)
+    def _(d):
+        to = peer(d)
+        for a in range(6):
+            in_copy(a, to, me, d).wait_send()
+        for i in range(2):
+            fw_copy(i, to, me, d).wait_send()
+        g_copy(to, me, d).wait_send()
+        gw_copy(to, d).wait_send()
+        for i in range(3):
+            gr_copy(i, to, me, d).wait_send()
+
+    cot_x.wait_send()
+    cot_core.wait_send()
+    cot_fwd.wait_send()
+    for j in range(1, ndp):
+        ad_copy(j).wait_send()
+
+
+def by_heads(
+    queries, key_rows, value_rows, query_tangent, key_tangent, value_tangent, out_weight, upstream
+):
+    n, ndp = lax.axis_size("seq"), lax.axis_size("dp")
+    tok, width = queries.shape[1:]
+    model = out_weight.shape[1]
+    full = n * tok
+    hd = HEAD_DIM
+    bf, f32 = jnp.bfloat16, jnp.float32
+    rows_dp = width // ndp
+    rows_own = rows_dp // n
+    any_spec = pl.BlockSpec(memory_space=pl.ANY)
+    vmem = pl.BlockSpec(memory_space=pltpu.VMEM)
+    dma = pltpu.SemaphoreType.DMA
+    flops = 2 * full * full * hd * 10 + 8 * tok * width * model
+    outs = pl.pallas_call(
+        functools.partial(fused_kernel, n, ndp),
+        out_shape=(
+            jax.ShapeDtypeStruct((tok, model), bf),
+            jax.ShapeDtypeStruct((tok, model), bf),
+            jax.ShapeDtypeStruct((rows_own, model), f32),
+            jax.ShapeDtypeStruct((tok, width), bf),
+            jax.ShapeDtypeStruct((tok, width), bf),
+            jax.ShapeDtypeStruct((tok, width), bf),
+        ),
+        in_specs=[any_spec] * 8,
+        out_specs=(vmem, vmem, vmem, any_spec, any_spec, any_spec),
+        scratch_shapes=[
+            pltpu.VMEM((full, 2 * hd), bf),
+            pltpu.VMEM((full, 2 * hd), bf),
+            pltpu.VMEM((full, 2 * hd), bf),
+            pltpu.VMEM((n // 2, full, 2 * tok), bf),
+            pltpu.VMEM((full, hd), bf),
+            pltpu.VMEM((full, hd), bf),
+            pltpu.VMEM((tok, width), bf),
+            pltpu.VMEM((tok, width), bf),
+            pltpu.VMEM((width, model), bf),
+            pltpu.VMEM((tok, model), bf),
+            pltpu.VMEM((ndp * tok, model), bf),
+            pltpu.VMEM((ndp * tok, rows_dp), bf),
+            pltpu.VMEM((tok, width), bf),
+            pltpu.VMEM((full, hd), bf),
+            pltpu.VMEM((full, hd), f32),
+            pltpu.VMEM((full, hd), bf),
+            pltpu.VMEM((full, hd), bf),
+            pltpu.VMEM((full, hd), bf),
+            pltpu.VMEM((rows_dp, model), bf),
+            pltpu.VMEM((n, rows_own, model), bf),
+            dma((6, n)), dma((6, n)), dma((2, n)), dma((2, n)), dma((n,)), dma((n,)),
+            dma((3, n)), dma((3, n)), dma((n,)), dma((n,)), dma((ndp,)), dma((ndp,)),
+            dma((ndp,)), dma((ndp,)), dma((2,)),
+        ],
+        compiler_params=pltpu.CompilerParams(
+            collective_id=0, has_side_effects=True, vmem_limit_bytes=52 * 1024 * 1024
+        ),
+        cost_estimate=pl.CostEstimate(
+            flops=flops, bytes_accessed=20 * tok * width, transcendentals=full * full
+        ),
+    )(
+        queries[0], key_rows[0], value_rows[0], query_tangent[0], key_tangent[0],
+        value_tangent[0], out_weight, upstream[0],
+    )
+    block, tan, gw, gq, gk, gv = outs
+    return block[None], tan[None], gw, gq[None], gk[None], gv[None]
+
+
 def solution(mesh):
+    fits = mesh.shape["seq"] == HEADS and mesh.shape["dp"] == 4
     placed = (
         P("dp", "seq", None),
         P("dp", "seq", None),
@@ -156,7 +550,7 @@
         P("dp", "seq", None),
     )
     return jax.shard_map(
-        per_device,
+        by_heads if fits else per_device,
         mesh=mesh,
         in_specs=placed,
         out_specs=(

time: 511 us -> 115 us (0.23)
  waiting for transfers between devices: 350 us -> 0 us
  Pallas kernels: 0 us -> 104 us
  blocking collectives: 61.1 us -> 0 us
  matrix products: 47.2 us -> 0 us
  local copies, waits for them, and re-layouts: 31 us -> 9.41 us
  between operations: 14.3 us -> 0.66 us
  other arithmetic: 6.06 us -> 0 us
    all_gather x6 -> x0, waiting for transfers between devices: 182 us -> none  [the longest x1 48.1 us: per_device(): key_piece = lax.all_gather(key_rows[0], 'seq', axis=0, tiled=True)]
    reduce_scatter x1 -> x0, waiting for transfers between devices: 167 us -> none  [per_device(): lax.psum_scatter(grad_factor * jnp.einsum('tk,te->ke', attn_flat, cotange...]
    pallas_call x0 -> x1, Pallas kernels: none -> 104 us  [by_heads(): pl.pallas_call(functools.partial(fused_kernel, n, ndp), out_shape=(jax.Sh...]
    all_gather x2 -> x0, blocking collectives: 61.1 us -> none  [the longest x1 30.6 us: per_device(): lax.all_gather(log_total.T, 'seq', axis=0, tiled=True)]
    dot_general x14 -> x0, matrix products: 47.2 us -> none  [the longest x1 5.83 us: per_device(): jnp.einsum('hqk,qhd->khd', dscore, query_heads, preferred_element_type=jn...]
    unnamed x29 -> x12, local copies, waits for them, and re-layouts: 18.3 us -> 9.41 us
    all_gather x2 -> x0, local copies, waits for them, and re-layouts: 7.93 us -> none  [the longest x1 3.98 us: per_device(): lax.all_gather(value_tangent[0], 'seq', axis=0, tiled=True)]
  transfers between devices with their start and end apart: 7 -> 0, of which waited for: 5 -> 0; matrix products, arithmetic and copies ran while one was open for 16% -> 0% of each run, Pallas kernels for 0% -> 0%
where the time goes in v1:
time: 115 us; the launch traced here: 114 us
  Pallas kernels  104 us (90%)
  local copies, waits for them, and re-layouts  9.41 us (8%)
    pallas_call x1, Pallas kernels, by_heads(): pl.pallas_call(functools.partial(fused_kernel, n, ndp), out_shape=(jax.Sh...  104 us
    unnamed x12, local copies, waits for them, and re-layouts  9.41 us

profile of v1, /device:TPU:0, one launch (start us, length us, event | category | flops | bytes accessed | tf_op | source)
XLA Modules:
  0.0 114.5 jit_solution(6924521164639151926)
XLA Ops:
  0.6 0.0 copy-start
  0.6 0.9 copy-done
  1.6 0.0 copy-start.1
  1.6 0.9 copy-done.1
  2.5 0.0 copy-start.2
  2.5 0.9 copy-done.2
  3.5 104.4 %shard_map.127 = (bf16[128,2048]{1,0:T(8,128)(2,1)}, bf16[128,2048]{1,0:T(8,128)(2,1)}, f32[32,2048]{1,0:T(8,128)S(1)}, bf16[128,1024]{1,0:T(8,128)(2,1)S(1)}, b...) custom-call(bf16[128,1024]{1,0:T(8,128)(2,1)S(1)} %bitcast.15, bf16[128,1024]{1,0:T(8,128)(2,1)S(1)} %bitcast.16, ...), custom_call_target="tpu_custom_call" | custom-call | flops 4831838208 | bytes 2621440 | tf_op jit(solution)/shard_map/pallas_call | solution.py:489
  107.9 1.9 %copy.20 = bf16[1,128,2048]{2,1,0:T(8,128)(2,1)} copy(bf16[1,128,2048]{2,1,0:T(8,128)(2,1)} %bitcast.19) | data formatting | bytes 1048576
  109.8 1.9 %copy.21 = bf16[1,128,2048]{2,1,0:T(8,128)(2,1)} copy(bf16[1,128,2048]{2,1,0:T(8,128)(2,1)} %bitcast.18) | data formatting | bytes 1048576
  111.7 0.7 copy.22
  112.4 0.7 copy.23
  113.1 0.7 copy.24
  113.8 0.7 copy.25
Async XLA Ops:
  0.6 1.0 copy-start
  1.6 0.9 copy-start.1
  2.5 0.9 copy-start.2

commit v2 on v1

--- a/solution.py
+++ b/solution.py
@@ -158,18 +158,20 @@
 
 def fused_kernel(
     n, ndp, q_ref, k_ref, v_ref, tq_ref, tk_ref, tv_ref, w_hbm, up_hbm,
-    block_ref, tan_ref, gw_ref, gq_out, gk_out, gv_out,
+    block_hbm, tan_hbm, gw_hbm, gq_out, gk_out, gv_out,
     qq, kk, vv, prob, attn_own, tan_own, attn_full, tan_full, w_ref, up_ref,
     cots, attn_dp, grad_loc, grad_own, gq_acc, gq_st, gk_st, gv_st, gw_st, gw_land,
+    e_ref, e_low, w_low, block_ref, tan_ref, gw_ref, cross_st, cross_land,
+    inv_ref, ut_ref, acc_ref,
     in_send, in_recv, fw_send, fw_recv, g_send, g_recv, gr_send, gr_recv,
-    gw_send, gw_recv, cot_send, cot_recv, ad_send, ad_recv, load_sem,
+    gw_send, gw_recv, cot_send, cot_recv, ad_send, ad_recv, load_sem, cross_send, cross_recv, out_sem,
 ):
     dp, me = lax.axis_index("dp"), lax.axis_index("seq")
     tok = q_ref.shape[0]
     hd = HEAD_DIM
     full = n * tok
-    rows_dp = gw_st.shape[0]
-    rows_own = rows_dp // n
+    rows_own = gw_st.shape[2]
+    rows_dp = n * rows_own
     scale = HEAD_DIM ** (-0.5)
     gw_scale = 1.0 / math.sqrt(ndp * full)
     dp_peers = [dp, dp + 1 - 2 * lax.rem(dp, 2), lax.rem(dp + 2, 4), 3 - dp]
@@ -179,6 +181,9 @@
 
     def source(d):
         return lax.rem(me + n - d, n)
+
+    def far_first(i):
+        return n // 2 + (1 - 2 * lax.rem(i, 2)) * ((i + 1) // 2)
 
     def at(i, size):
         return pl.ds(pl.multiple_of(i * size, size), size)
@@ -216,8 +221,9 @@
         in_local(a).start()
     pl.semaphore_wait(barrier, n - 1 + ndp - 1)
     for a in range(6):
-        @pl.loop(1, n)
-        def _(d):
+        @pl.loop(0, n - 1)
+        def _(i):
+            d = far_first(i)
             in_copy(a, peer(d), me, d).start()
     load_w.start()
     load_up.start()
@@ -228,9 +234,6 @@
         @pl.loop(1, n)
         def _(d):
             in_copy(a, source(d), source(d), d).wait_recv()
-
-    for a in range(6):
-        in_wait(a)
 
     def fw_copy(i, to, owner, d):
         src, dst = ((attn_own, attn_full), (tan_own, tan_full))[i]
@@ -250,25 +253,51 @@
     span = 2 * tok
     parts = n // 2
 
+    in_wait(0)
+    in_wait(1)
+
     @pl.loop(0, parts)
-    def _(j):
-        p = lax.rem(me // 2 + 1 + j, parts)
+    def _(p):
         rows = at(p, span)
-        q2 = qq[rows, :]
-        s = dotf(q2[:, hd:], kk[:, :hd], NT)
+        s = dotf(qq[rows, hd:], kk[:, :hd], NT)
         e = jnp.exp((s - jnp.max(s, axis=1, keepdims=True)) * scale)
-        wgt = e * dotf(q2, kk[...], NT)
-        total = jnp.sum(e, axis=1, keepdims=True)
-        tan_total = jnp.sum(wgt, axis=1, keepdims=True) * scale
-        inv = 1.0 / total
-        both = dotf(e.astype(jnp.bfloat16), vv[...])
-        acc_t = dotf(wgt.astype(jnp.bfloat16), vv[:, :hd]) * scale + both[:, hd:]
-        wide = both[:, :hd] * inv
-        attn_own[rows, :] = wide.astype(jnp.bfloat16)
-        tan_own[rows, :] = ((acc_t - wide * tan_total) * inv).astype(jnp.bfloat16)
+        inv = 1.0 / jnp.sum(e, axis=1, keepdims=True)
+        inv_ref[rows, :] = inv
+        e_ref[rows, :] = e
+        e_low[rows, :] = e.astype(jnp.bfloat16)
         pb = (e * inv).astype(jnp.bfloat16)
         for c in range(parts):
             prob[c, rows, :] = pb[:, c * span:(c + 1) * span]
+
+    in_wait(2)
+    in_wait(3)
+
+    @pl.loop(0, parts)
+    def _(p):
+        rows = at(p, span)
+        wgt = e_ref[rows, :] * dotf(qq[rows, :], kk[...], NT)
+        ut_ref[rows, :] = jnp.sum(wgt, axis=1, keepdims=True) * scale
+        w_low[rows, :] = wgt.astype(jnp.bfloat16)
+
+    in_wait(4)
+
+    @pl.loop(0, parts)
+    def _(p):
+        rows = at(p, span)
+        inv = inv_ref[rows, :]
+        wide = dotf(e_low[rows, :], vv[:, :hd]) * inv
+        attn_own[rows, :] = wide.astype(jnp.bfloat16)
+        part = dotf(w_low[rows, :], vv[:, :hd]) * scale
+        acc_ref[rows, :] = part - wide * ut_ref[rows, :]
+
+    in_wait(5)
+
+    @pl.loop(0, parts)
+    def _(j):
+        p = lax.rem(me // 2 + parts // 2 + j, parts)
+        rows = at(p, span)
+        acc_t = acc_ref[rows, :] + dotf(e_low[rows, :], vv[:, hd:])
+        tan_own[rows, :] = (acc_t * inv_ref[rows, :]).astype(jnp.bfloat16)
         for half in range(2):
             owner = 2 * p + half
             d = lax.rem(owner + n - me, n)
@@ -276,12 +305,17 @@
             @pl.when(d != 0)
             def _():
                 fw_copy(1, owner, me, d).start()
-                fw_copy(0, owner, me, d).start()
 
             @pl.when(d == 0)
             def _():
                 fw_local(1).start()
-                fw_local(0).start()
+
+    fw_local(0).start()
+
+    @pl.loop(0, n - 1)
+    def _(i):
+        d = far_first(i)
+        fw_copy(0, peer(d), me, d).start()
 
     load_w.wait()
     load_up.wait()
@@ -296,6 +330,10 @@
     fw_wait(1)
     ty = dotf(tan_full[...], w_ref[...])
     tan_ref[...] = ty.astype(jnp.bfloat16)
+    tan_out = pltpu.make_async_copy(tan_ref, tan_hbm, out_sem.at[0])
+    block_out = pltpu.make_async_copy(block_ref, block_hbm, out_sem.at[1])
+    gw_out = pltpu.make_async_copy(gw_ref, gw_hbm, out_sem.at[2])
+    tan_out.start()
     cot = (ty + up_ref[...].astype(jnp.float32)).astype(jnp.bfloat16)
     cots[pl.ds(0, tok), :] = cot
     grad_loc[...] = dotf(cot, w_ref[...], NT).astype(jnp.bfloat16)
@@ -313,8 +351,9 @@
     )
     g_local.start()
 
-    @pl.loop(1, n)
-    def _(d):
+    @pl.loop(0, n - 1)
+    def _(i):
+        d = far_first(i)
         g_copy(peer(d), me, d).start()
 
     def cot_copy(src_slot, dst_slot, to):
@@ -348,6 +387,7 @@
         ad_copy(j).start()
     ad_local.start()
     block_ref[...] = dotf(attn_full[...], w_ref[...]).astype(jnp.bfloat16)
+    block_out.start()
 
     g_local.wait()
 
@@ -379,7 +419,7 @@
     gq_acc[...] = jnp.zeros_like(gq_acc)
 
     def back_chunk(j):
-        p = lax.rem(me // 2 + 1 + j, parts)
+        p = lax.rem(me // 2 + parts // 2 + j, parts)
         rows = at(p, span)
         pc = prob[p]
         dprob = dotf(g_all, vv[rows, :hd], NT)
@@ -401,13 +441,26 @@
                 gr_local(0).start()
                 gr_local(1).start()
 
-    def gw_copy(to, d):
+    half_n = n // 2
+    spot, side = lax.rem(me, half_n), me // half_n
+
+    def half_peer(d):
+        return lax.rem(spot + d, half_n)
+
+    def gw_copy(d):
+        to = half_peer(d)
         return pltpu.make_async_remote_copy(
-            src_ref=gw_st.at[at(to, rows_own), :],
+            src_ref=gw_st.at[:, to],
             dst_ref=gw_land.at[d],
             send_sem=gw_send.at[d], recv_sem=gw_recv.at[d],
-            device_id=(dp, to), device_id_type=MESH,
-        )
+            device_id=(dp, side * half_n + to), device_id_type=MESH,
+        )
+
+    cross = pltpu.make_async_remote_copy(
+        src_ref=cross_st, dst_ref=cross_land,
+        send_sem=cross_send.at[0], recv_sem=cross_recv.at[0],
+        device_id=(dp, peer(half_n)), device_id_type=MESH,
+    )
 
     first = parts // 2
 
@@ -422,11 +475,12 @@
     for j in range(1, ndp):
         ad_copy(j).wait_recv()
     cot_fwd.wait_recv()
-    gw_st[...] = (dotf(attn_dp[...], cots[...], TN) * gw_scale).astype(jnp.bfloat16)
-
-    @pl.loop(1, n)
-    def _(d):
-        gw_copy(peer(d), d).start()
+    gw_part = (dotf(attn_dp[...], cots[...], TN) * gw_scale).astype(jnp.bfloat16)
+    for b in range(n):
+        gw_st[b // half_n, b % half_n] = gw_part[b * rows_own:(b + 1) * rows_own, :]
+
+    for d in range(1, half_n):
+        gw_copy(d).start()
 
     @pl.loop(first, parts)
     def _(j):
@@ -435,15 +489,22 @@
     gq_st[...] = (gq_acc[...] * scale).astype(jnp.bfloat16)
     gr_local(2).start()
 
-    @pl.loop(1, n)
-    def _(d):
+    @pl.loop(0, n - 1)
+    def _(i):
+        d = far_first(i)
         gr_copy(2, peer(d), me, d).start()
 
-    gw_total = gw_st[at(me, rows_own), :].astype(jnp.float32)
-    for d in range(1, n):
-        gw_copy(source(d), d).wait_recv()
-        gw_total = gw_total + gw_land[d].astype(jnp.float32)
-    gw_ref[...] = gw_total
+    own = gw_st[side, spot].astype(jnp.float32)
+    other = gw_st[1 - side, spot].astype(jnp.float32)
+    for d in range(1, half_n):
+        gw_copy(d).wait_recv()
+        own = own + gw_land[d, side].astype(jnp.float32)
+        other = other + gw_land[d, 1 - side].astype(jnp.float32)
+    cross_st[...] = other.astype(jnp.bfloat16)
+    cross.start()
+    cross.wait_recv()
+    gw_ref[...] = own + cross_land[...].astype(jnp.float32)
+    gw_out.start()
 
     for i in range(3):
         gr_local(i).wait()
@@ -460,15 +521,37 @@
         for i in range(2):
             fw_copy(i, to, me, d).wait_send()
         g_copy(to, me, d).wait_send()
-        gw_copy(to, d).wait_send()
         for i in range(3):
             gr_copy(i, to, me, d).wait_send()
 
+    for d in range(1, half_n):
+        gw_copy(d).wait_send()
+    cross.wait_send()
+    tan_out.wait()
+    block_out.wait()
+    gw_out.wait()
     cot_x.wait_send()
     cot_core.wait_send()
     cot_fwd.wait_send()
     for j in range(1, ndp):
         ad_copy(j).wait_send()
+
+
+def hand_over(*refs):
+    count = (len(refs) - 2) // 3
+    held = refs[2 * count:3 * count]
+    in_sem, out_sem = refs[-2:]
+    loads = [pltpu.make_async_copy(refs[i], held[i], in_sem.at[i]) for i in range(count)]
+    stores = [
+        pltpu.make_async_copy(held[i], refs[count + i], out_sem.at[i]) for i in range(count)
+    ]
+    for load in loads:
+        load.start()
+    for load, store in zip(loads, stores):
+        load.wait()
+        store.start()
+    for store in stores:
+        store.wait()
 
 
 def by_heads(
@@ -482,8 +565,7 @@
     bf, f32 = jnp.bfloat16, jnp.float32
     rows_dp = width // ndp
     rows_own = rows_dp // n
-    any_spec = pl.BlockSpec(memory_space=pl.ANY)
-    vmem = pl.BlockSpec(memory_space=pltpu.VMEM)
+    any_spec = pl.BlockSpec(memory_space=pltpu.HBM)
     dma = pltpu.SemaphoreType.DMA
     flops = 2 * full * full * hd * 10 + 8 * tok * width * model
     outs = pl.pallas_call(
@@ -497,7 +579,7 @@
             jax.ShapeDtypeStruct((tok, width), bf),
         ),
         in_specs=[any_spec] * 8,
-        out_specs=(vmem, vmem, vmem, any_spec, any_spec, any_spec),
+        out_specs=(any_spec,) * 6,
         scratch_shapes=[
             pltpu.VMEM((full, 2 * hd), bf),
             pltpu.VMEM((full, 2 * hd), bf),
@@ -517,14 +599,26 @@
             pltpu.VMEM((full, hd), bf),
             pltpu.VMEM((full, hd), bf),
             pltpu.VMEM((full, hd), bf),
-            pltpu.VMEM((rows_dp, model), bf),
-            pltpu.VMEM((n, rows_own, model), bf),
+            pltpu.VMEM((2, n // 2, rows_own, model), bf),
+            pltpu.VMEM((n // 2, 2, rows_own, model), bf),
+            pltpu.VMEM((full, full), f32),
+            pltpu.VMEM((full, full), bf),
+            pltpu.VMEM((full, full), bf),
+            pltpu.VMEM((tok, model), bf),
+            pltpu.VMEM((tok, model), bf),
+            pltpu.VMEM((rows_own, model), f32),
+            pltpu.VMEM((rows_own, model), bf),
+            pltpu.VMEM((rows_own, model), bf),
+            pltpu.VMEM((full, 1), f32),
+            pltpu.VMEM((full, 1), f32),
+            pltpu.VMEM((full, hd), f32),
             dma((6, n)), dma((6, n)), dma((2, n)), dma((2, n)), dma((n,)), dma((n,)),
             dma((3, n)), dma((3, n)), dma((n,)), dma((n,)), dma((ndp,)), dma((ndp,)),
             dma((ndp,)), dma((ndp,)), dma((2,)),
+            dma((1,)), dma((1,)), dma((3,)),
         ],
         compiler_params=pltpu.CompilerParams(
-            collective_id=0, has_side_effects=True, vmem_limit_bytes=52 * 1024 * 1024
+            collective_id=0, has_side_effects=True, vmem_limit_bytes=60 * 1024 * 1024
         ),
         cost_estimate=pl.CostEstimate(
             flops=flops, bytes_accessed=20 * tok * width, transcendentals=full * full
@@ -533,7 +627,13 @@
         queries[0], key_rows[0], value_rows[0], query_tangent[0], key_tangent[0],
         value_tangent[0], out_weight, upstream[0],
     )
-    block, tan, gw, gq, gk, gv = outs
+    block, tan, gw, gq, gk, gv = pl.pallas_call(
+        hand_over,
+        out_shape=tuple(jax.ShapeDtypeStruct(o.shape, o.dtype) for o in outs),
+        in_specs=[any_spec] * 6,
+        out_specs=(any_spec,) * 6,
+        scratch_shapes=[pltpu.VMEM(o.shape, o.dtype) for o in outs] + [dma((6,)), dma((6,))],
+    )(*outs)
     return block[None], tan[None], gw, gq[None], gk[None], gv[None]
 
 

time: 115 us -> 98.7 us (0.86)
  local copies, waits for them, and re-layouts: 9.41 us -> 0 us
  Pallas kernels: 104 us -> 96.9 us
    pallas_call x1, Pallas kernels: 104 us -> 94.5 us  [by_heads(): pl.pallas_call(functools.partial(fused_kernel, n, ndp), out_shape=(jax.Sh...]
    unnamed x12 -> x0, local copies, waits for them, and re-layouts: 9.41 us -> none
    pallas_call x0 -> x1, Pallas kernels: none -> 2.45 us  [by_heads(): pl.pallas_call(hand_over, out_shape=tuple((jax.ShapeDtypeStruct(o.shape,...]
where the time goes in v2:
time: 98.7 us; the launch traced here: 97.6 us
  Pallas kernels  96.9 us (98%)
    pallas_call x1, Pallas kernels, by_heads(): pl.pallas_call(functools.partial(fused_kernel, n, ndp), out_shape=(jax.Sh...  94.5 us
    pallas_call x1, Pallas kernels, by_heads(): pl.pallas_call(hand_over, out_shape=tuple((jax.ShapeDtypeStruct(o.shape,...  2.45 us

profile of v2, /device:TPU:0, one launch (start us, length us, event | category | flops | bytes accessed | tf_op | source)
XLA Modules:
  0.0 97.6 jit_solution(13675957520972014900)
XLA Ops:
  0.6 94.5 %shard_map.127 = (bf16[128,2048]{1,0:T(8,128)(2,1)}, bf16[128,2048]{1,0:T(8,128)(2,1)}, f32[32,2048]{1,0:T(8,128)}, bf16[128,1024]{1,0:T(8,128)(2,1)}, bf16[128,...) custom-call(bf16[128,1024]{1,0:T(8,128)(2,1)} %bitcast.15, bf16[128,1024]{1,0:T(8,128)(2,1)} %bitcast.16, ...), custom_call_target="tpu_custom_call" | custom-call | flops 4831838208 | bytes 2621440 | tf_op jit(solution)/shard_map/pallas_call | solution.py:571
  95.1 2.5 %shard_map.128 = (bf16[128,2048]{1,0:T(8,128)(2,1)}, bf16[128,2048]{1,0:T(8,128)(2,1)}, f32[32,2048]{1,0:T(8,128)}, bf16[128,1024]{1,0:T(8,128)(2,1)}, bf16[128,...) custom-call(bf16[128,2048]{1,0:T(8,128)(2,1)} %get-tuple-element.18.refs_0_, bf16[128,2048]{1,0:T(8,128)(2,1)} %get-tuple-element.19.refs_1_, ...), custom_call_target="tpu_custom_call" | custom-call | tf_op jit(solution)/shard_map/pallas_call | solution.py:630

commit v3 on v2

--- a/solution.py
+++ b/solution.py
@@ -336,6 +336,21 @@
     tan_out.start()
     cot = (ty + up_ref[...].astype(jnp.float32)).astype(jnp.bfloat16)
     cots[pl.ds(0, tok), :] = cot
+
+    def cot_copy(src_slot, dst_slot, to):
+        return pltpu.make_async_remote_copy(
+            src_ref=cots.at[pl.ds(src_slot * tok, tok), :],
+            dst_ref=cots.at[pl.ds(dst_slot * tok, tok), :],
+            send_sem=cot_send.at[dst_slot], recv_sem=cot_recv.at[dst_slot],
+            device_id=(to, me), device_id_type=MESH,
+        )
+
+    cot_x = cot_copy(0, 2, dp_peers[2])
+    cot_core = cot_copy(0, 1, dp_peers[1])
+    cot_fwd = cot_copy(2, 3, dp_peers[1])
+    cot_x.start()
+    cot_core.start()
+
     grad_loc[...] = dotf(cot, w_ref[...], NT).astype(jnp.bfloat16)
 
     def g_copy(to, owner, d):
@@ -355,20 +370,6 @@
     def _(i):
         d = far_first(i)
         g_copy(peer(d), me, d).start()
-
-    def cot_copy(src_slot, dst_slot, to):
-        return pltpu.make_async_remote_copy(
-            src_ref=cots.at[pl.ds(src_slot * tok, tok), :],
-            dst_ref=cots.at[pl.ds(dst_slot * tok, tok), :],
-            send_sem=cot_send.at[dst_slot], recv_sem=cot_recv.at[dst_slot],
-            device_id=(to, me), device_id_type=MESH,
-        )
-
-    cot_x = cot_copy(0, 2, dp_peers[2])
-    cot_core = cot_copy(0, 1, dp_peers[1])
-    cot_fwd = cot_copy(2, 3, dp_peers[1])
-    cot_x.start()
-    cot_core.start()
 
     fw_wait(0)
 

time: 98.7 us -> 96.8 us (0.981)
  Pallas kernels: 96.9 us -> 95.3 us
    pallas_call x1, Pallas kernels: 94.5 us -> 92.9 us  [by_heads(): pl.pallas_call(functools.partial(fused_kernel, n, ndp), out_shape=(jax.Sh...]
where the time goes in v3:
time: 96.8 us; the launch traced here: 96 us
  Pallas kernels  95.3 us (98%)
    pallas_call x1, Pallas kernels, by_heads(): pl.pallas_call(functools.partial(fused_kernel, n, ndp), out_shape=(jax.Sh...  92.9 us
    pallas_call x1, Pallas kernels, by_heads(): pl.pallas_call(hand_over, out_shape=tuple((jax.ShapeDtypeStruct(o.shape,...  2.45 us

profile of v3, /device:TPU:0, one launch (start us, length us, event | category | flops | bytes accessed | tf_op | source)
XLA Modules:
  0.0 96.0 jit_solution(15564706288236357577)
XLA Ops:
  0.6 92.9 %shard_map.127 = (bf16[128,2048]{1,0:T(8,128)(2,1)}, bf16[128,2048]{1,0:T(8,128)(2,1)}, f32[32,2048]{1,0:T(8,128)}, bf16[128,1024]{1,0:T(8,128)(2,1)}, bf16[128,...) custom-call(bf16[128,1024]{1,0:T(8,128)(2,1)} %bitcast.15, bf16[128,1024]{1,0:T(8,128)(2,1)} %bitcast.16, ...), custom_call_target="tpu_custom_call" | custom-call | flops 4831838208 | bytes 2621440 | tf_op jit(solution)/shard_map/pallas_call | solution.py:572
  93.5 2.5 %shard_map.128 = (bf16[128,2048]{1,0:T(8,128)(2,1)}, bf16[128,2048]{1,0:T(8,128)(2,1)}, f32[32,2048]{1,0:T(8,128)}, bf16[128,1024]{1,0:T(8,128)(2,1)}, bf16[128,...) custom-call(bf16[128,2048]{1,0:T(8,128)(2,1)} %get-tuple-element.18.refs_0_, bf16[128,2048]{1,0:T(8,128)(2,1)} %get-tuple-element.19.refs_1_, ...), custom_call_target="tpu_custom_call" | custom-call | tf_op jit(solution)/shard_map/pallas_call | solution.py:631

commit v4 on v3

--- a/solution.py
+++ b/solution.py
@@ -310,6 +310,17 @@
             def _():
                 fw_local(1).start()
 
+    load_w.wait()
+    load_up.wait()
+
+    def fw_wait(i):
+        fw_local(i).wait()
+
+        @pl.loop(1, n)
+        def _(d):
+            fw_copy(i, source(d), source(d), d).wait_recv()
+
+    fw_wait(1)
     fw_local(0).start()
 
     @pl.loop(0, n - 1)
@@ -317,17 +328,6 @@
         d = far_first(i)
         fw_copy(0, peer(d), me, d).start()
 
-    load_w.wait()
-    load_up.wait()
-
-    def fw_wait(i):
-        fw_local(i).wait()
-
-        @pl.loop(1, n)
-        def _(d):
-            fw_copy(i, source(d), source(d), d).wait_recv()
-
-    fw_wait(1)
     ty = dotf(tan_full[...], w_ref[...])
     tan_ref[...] = ty.astype(jnp.bfloat16)
     tan_out = pltpu.make_async_copy(tan_ref, tan_hbm, out_sem.at[0])

time: 96.8 us -> 98.1 us (1.013)
  Pallas kernels: 95.3 us -> 96.5 us
    pallas_call x1, Pallas kernels: 92.9 us -> 94 us  [by_heads(): pl.pallas_call(functools.partial(fused_kernel, n, ndp), out_shape=(jax.Sh...]
where the time goes in v4:
time: 98.1 us; the launch traced here: 97.1 us
  Pallas kernels  96.5 us (98%)
    pallas_call x1, Pallas kernels, by_heads(): pl.pallas_call(functools.partial(fused_kernel, n, ndp), out_shape=(jax.Sh...  94 us
    pallas_call x1, Pallas kernels, by_heads(): pl.pallas_call(hand_over, out_shape=tuple((jax.ShapeDtypeStruct(o.shape,...  2.45 us

profile of v4, /device:TPU:0, one launch (start us, length us, event | category | flops | bytes accessed | tf_op | source)
XLA Modules:
  0.0 97.1 jit_solution(11989041463446787528)
XLA Ops:
  0.6 94.0 %shard_map.127 = (bf16[128,2048]{1,0:T(8,128)(2,1)}, bf16[128,2048]{1,0:T(8,128)(2,1)}, f32[32,2048]{1,0:T(8,128)}, bf16[128,1024]{1,0:T(8,128)(2,1)}, bf16[128,...) custom-call(bf16[128,1024]{1,0:T(8,128)(2,1)} %bitcast.15, bf16[128,1024]{1,0:T(8,128)(2,1)} %bitcast.16, ...), custom_call_target="tpu_custom_call" | custom-call | flops 4831838208 | bytes 2621440 | tf_op jit(solution)/shard_map/pallas_call | solution.py:572
  94.7 2.5 %shard_map.128 = (bf16[128,2048]{1,0:T(8,128)(2,1)}, bf16[128,2048]{1,0:T(8,128)(2,1)}, f32[32,2048]{1,0:T(8,128)}, bf16[128,1024]{1,0:T(8,128)(2,1)}, bf16[128,...) custom-call(bf16[128,2048]{1,0:T(8,128)(2,1)} %get-tuple-element.18.refs_0_, bf16[128,2048]{1,0:T(8,128)(2,1)} %get-tuple-element.19.refs_1_, ...), custom_call_target="tpu_custom_call" | custom-call | tf_op jit(solution)/shard_map/pallas_call | solution.py:631
